TPU v7x, 32 devices: a whole 2x2x4 slice. The times are simulated.
32 devices in a mesh: dp: 8 (over y, x, core), tp: 4 (over z).
Axes of the slice: x: 2, y: 2, z: 4, core: 2. Of those that a mesh axis runs over, the one named last changes fastest.
Arguments:
- hidden_states: bfloat16 [4096, 3, 4096], P('dp', None, 'tp'), may hold values from -6 to 6
- fc_weight: bfloat16 [4096, 3, 4096], P('dp', None, 'tp'), may hold values from -0.0546875 to 0.0546875
- norm_gain: float32 [4096], replicated, may hold values from 0.1 to 1.9
- upstream: bfloat16 [4096, 4096], P(('dp', 'tp')), may hold values from -0.1875 to 0.1875
- lengths: int32 [32], P(('dp', 'tp')), may hold values from 1 to 128, as said below
Outputs:
- normed: bfloat16 [4096, 4096], P(('dp', 'tp'))
- grad_weight: float32 [4096, 3, 4096], P('dp', None, 'tp')
- grad_gain: float32 [4096], replicated
Inputs may be any that keep to these rules, and one draw needn't show every extreme that they name: `lengths`: some sample carries loss at all 128 positions.
All inputs are finite; a program needn't handle non-finite values.
Results may differ from a plain program's by a relative error of at most 0.014.
Values may be sent and summed in bfloat16 or wider, within the bound.
A program may use at most 128 MiB of HBM per device.

v0:
```python
import jax
import jax.numpy as jnp
from jax import lax
from jax.sharding import PartitionSpec as P


def body(hidden_states, fc_weight, norm_gain, upstream, lengths):
    tok_group, layers, slab_width = hidden_states.shape
    tok_dev, draft_width = upstream.shape
    flat_hidden = hidden_states.reshape(tok_group, layers * slab_width)
    contract_last = (((1,), (1,)), ((), ()))
    contract_first = (((0,), (0,)), ((), ()))
    weight_piece = lax.all_gather(fc_weight, "dp", axis=0, tiled=True)
    flat_piece = weight_piece.reshape(weight_piece.shape[0], layers * slab_width)
    slab_sums = lax.dot_general(
        flat_hidden, flat_piece, contract_last, preferred_element_type=jnp.float32
    )
    merged = lax.psum_scatter(
        slab_sums.astype(jnp.bfloat16), "tp", scatter_dimension=0, tiled=True
    ).astype(jnp.float32)
    squares = jnp.mean(merged * merged, axis=1, keepdims=True)
    inverse = lax.rsqrt(squares + 1e-05)
    scaled = merged * inverse
    normed = (scaled * norm_gain).astype(jnp.bfloat16)
    positions = lax.broadcasted_iota(jnp.int32, (tok_dev, 1), 0)
    live_mask = (positions < lengths[0]).astype(jnp.float32)
    incoming = upstream.astype(jnp.float32) * live_mask
    grad_gain = lax.psum(jnp.sum(incoming * scaled, axis=0), ("dp", "tp"))
    grad_scaled = incoming * norm_gain
    projection = jnp.mean(grad_scaled * scaled, axis=1, keepdims=True)
    grad_merged = (inverse * (grad_scaled - scaled * projection)).astype(jnp.bfloat16)
    grad_group = lax.all_gather(grad_merged, "tp", axis=0, tiled=True)
    product = lax.dot_general(
        grad_group, flat_hidden, contract_first, preferred_element_type=jnp.float32
    )
    grad_weight = lax.psum_scatter(
        product.reshape(fc_weight.shape[0] * lax.axis_size("dp"), layers, slab_width).astype(
            jnp.bfloat16
        ),
        "dp",
        scatter_dimension=0,
        tiled=True,
    ).astype(jnp.float32)
    return (normed, grad_weight, grad_gain)


def solution(mesh):
    return jax.shard_map(
        body,
        mesh=mesh,
        in_specs=(
            P("dp", None, "tp"),
            P("dp", None, "tp"),
            P(),
            P(("dp", "tp"), None),
            P(("dp", "tp")),
        ),
        out_specs=(P(("dp", "tp"), None), P("dp", None, "tp"), P()),
        check_vma=False,
    )
```

profile of v0, /device:TPU:0, one launch (start us, length us, event | category | flops | bytes accessed | tf_op | source)
XLA Modules:
  0.0 508.2 jit_solution(8107644856751377494)
XLA Ops:
  7.2 0.0 copy-start.2
  7.2 0.0 all-gather.3.cloned.1.call-start
  7.2 0.7 all-gather.3.cloned.1.call-update
  7.9 0.0 reduce-scatter.3.cloned.1.call-start
  8.0 130.0 %all-gather.3.cloned.1.call-done = bf16[4096,3,1024]{2,0,1:T(8,128)(2,1)} async-done(((bf16[512,3,1024]{2,0,1:T(8,128)(2,1)}), bf16[4096,3,1024]{2,0,1:T(8,128)(2,1)}) %all-gather.3.cloned.1.call-update) | async-done | bytes 25165840 | tf_op jit(solution)/shard_map/all_gather | solution.py:13
  138.0 0.0 copy-done.2
  138.0 19.3 %bitcast_convert_fusion = bf16[512,4096]{1,0:T(8,128)(2,1)} fusion(bf16[512,3,1024]{2,0,1:T(8,128)(2,1)S(1)} %copy-done.2, bf16[4096,3,1024]{2,0,1:T(8,128)(2,1)} %all-gather.3.cloned.1.call-done), kind=kOutput, calls=%fused_computation.1 | convolution fusion | flops 12886999040 | bytes 32505856 | tf_op jit(solution)/shard_map/dot_general | solution.py:15
  157.3 0.0 copy-start.1
  157.3 0.0 copy-start.3
  157.3 0.0 reduce-scatter.3.cloned.1.call-update
  157.3 0.0 all-gather.5.cloned.1.call-start
  158.1 76.1 %reduce-scatter.3.cloned.1.call-done = bf16[128,4096]{1,0:T(8,128)(2,1)} async-done(((bf16[512,4096]{1,0:T(8,128)(2,1)}), bf16[128,4096]{1,0:T(8,128)(2,1)}) %reduce-scatter.3.cloned.1.call-update) | async-done | bytes 1048592 | tf_op jit(solution)/shard_map/reduce_scatter | solution.py:18
  234.2 0.0 copy-start
  234.2 1.6 fusion.12
  235.8 0.0 copy-done.1
  235.8 0.0 copy-done.3
  235.8 2.0 fusion.11
  237.9 0.0 copy-done
  237.9 2.2 fusion.10
  240.1 0.0 all-gather.5.cloned.1.call-update
  240.1 0.2 reduce-scatter.5.cloned.1.call-start
  240.3 3.2 copy.9
  243.5 78.0 %all-gather.5.cloned.1.call-done = bf16[512,4096]{1,0:T(8,128)(2,1)} async-done(((bf16[128,4096]{1,0:T(8,128)(2,1)}), bf16[512,4096]{1,0:T(8,128)(2,1)}) %all-gather.5.cloned.1.call-update) | async-done | bytes 4194320 | tf_op jit(solution)/shard_map/all_gather | solution.py:32
  321.5 19.2 %convolution_convert_fusion = bf16[4096,3,1024]{2,0,1:T(8,128)(2,1)} fusion(bf16[512,4096]{1,0:T(8,128)(2,1)} %all-gather.5.cloned.1.call-done, bf16[512,3,1024]{0,2,1:T(8,128)(2,1)S(1)} %copy.9), kind=kOutput, calls=%fused_computation | convolution fusion | flops 12897484800 | bytes 32505856 | tf_op jit(solution)/shard_map/dot_general | solution.py:33
  340.7 0.0 reduce-scatter.5.cloned.1.call-update
  340.7 38.9 %psum.7 = f32[4096]{0:T(1024)} all-reduce(f32[4096]{0:T(1024)S(1)} %get-tuple-element.3), channel_id=1, replica_groups=mesh['dp'=8,'tp'=4] {'dp','tp'}, use_global_device_ids=true, to_apply=%region_5.0 | all-reduce | flops 4096 | bytes 32768 | tf_op jit(solution)/shard_map/psum | solution.py:28
  379.6 116.7 %reduce-scatter.5.cloned.1.call-done = bf16[512,3,1024]{2,0,1:T(8,128)(2,1)} async-done(((bf16[4096,3,1024]{2,0,1:T(8,128)(2,1)}), bf16[512,3,1024]{2,0,1:T(8,128)(2,1)}) %reduce-scatter.5.cloned.1.call-update) | async-done | bytes 3145744 | tf_op jit(solution)/shard_map/reduce_scatter | solution.py:36
  496.3 5.3 %convert_element_type.36 = f32[512,3,1024]{2,0,1:T(8,128)} convert(bf16[512,3,1024]{2,0,1:T(8,128)(2,1)} %reduce-scatter.5.cloned.1.call-done) | non-fusion elementwise | flops 1572864 | bytes 9437184 | tf_op jit(solution)/shard_map/convert_element_type | solution.py:43
  (3 shorter events, 0.0 us)
Async XLA Ops:
  7.2 130.8 %copy-start.2 = (bf16[512,3,1024]{2,0,1:T(8,128)(2,1)S(1)}, bf16[512,3,1024]{2,0,1:T(8,128)(2,1)}, u32[]{:S(2)}) copy-start(bf16[512,3,1024]{2,0,1:T(8,128)(2,1)} %param.5) | copy-start | bytes 9437188
  7.2 130.8 %all-gather.3.cloned.1.call-start = ((), (), s32[]{:S(2)}) async-start(), calls=%async_computation.2 | async-start | bytes 28311552 | tf_op jit(solution)/shard_map/all_gather | solution.py:13
  7.9 226.3 %reduce-scatter.3.cloned.1.call-start = ((), (), s32[]{:S(2)}) async-start(), calls=%async_computation.3 | async-start | bytes 5242880 | tf_op jit(solution)/shard_map/reduce_scatter | solution.py:18
  157.3 78.6 %copy-start.1 = (bf16[128,4096]{1,0:T(8,128)(2,1)S(1)}, bf16[128,4096]{1,0:T(8,128)(2,1)}, u32[]{:S(2)}) copy-start(bf16[128,4096]{1,0:T(8,128)(2,1)} %param.8) | copy-start | bytes 3145732
  157.3 78.6 %copy-start.3 = (f32[4096]{0:T(1024)S(1)}, f32[4096]{0:T(1024)}, u32[]{:S(2)}) copy-start(f32[4096]{0:T(1024)} %param.7) | copy-start | bytes 49156
  157.3 164.2 %all-gather.5.cloned.1.call-start = ((), (), s32[]{:S(2)}) async-start(), calls=%async_computation.4 | async-start | bytes 5242880 | tf_op jit(solution)/shard_map/all_gather | solution.py:32
  234.2 3.7 copy-start
  240.1 256.2 %reduce-scatter.5.cloned.1.call-start = ((), (), s32[]{:S(2)}) async-start(), calls=%async_computation.5 | async-start | bytes 28311552 | tf_op jit(solution)/shard_map/reduce_scatter | solution.py:36
Sparse Core Ops, SparseCore 0:
  9.9 128.0 all-gather.2
  157.4 76.7 reduce-scatter.2
  240.2 81.2 all-gather.4
  340.9 155.3 reduce-scatter.4
where the time goes:
time: 509 us; the launch traced here: 508 us
  waiting for transfers between devices  402 us (79%)
  blocking collectives  38.9 us (8%)
  matrix products  38.5 us (8%)
  between operations  14.5 us (3%)
  other arithmetic  11.2 us (2%)
    all_gather x1, waiting for transfers between devices, body(): weight_piece = lax.all_gather(fc_weight, 'dp', axis=0, tiled=True)  130 us
    reduce_scatter x1, waiting for transfers between devices, body(): lax.psum_scatter(product.reshape(fc_weight.shape[0] * lax.axis_size('dp')...  117 us
    all_gather x1, waiting for transfers between devices, body(): grad_group = lax.all_gather(grad_merged, 'tp', axis=0, tiled=True)  78 us
    reduce_scatter x1, waiting for transfers between devices, body(): lax.psum_scatter(slab_sums.astype(jnp.bfloat16), 'tp', scatter_dimension=...  76.1 us
    psum x1, blocking collectives, body(): grad_gain = lax.psum(jnp.sum(incoming * scaled, axis=0), ('dp', 'tp'))  38.9 us
    dot_general x1, matrix products, body(): lax.dot_general(flat_hidden, flat_piece, contract_last, preferred_element...  19.3 us
    dot_general x1, matrix products, body(): lax.dot_general(grad_group, flat_hidden, contract_first, preferred_elemen...  19.2 us
  transfers between devices with their start and end apart: 4, of which 4 were waited for; matrix products, arithmetic and copies ran while one was open for 1% of the time, Pallas kernels for 0%

commit v1 on v0

v1 whole, which is shorter than its diff:
```python
import functools

import jax
import jax.numpy as jnp
from jax import lax
from jax.experimental import pallas as pl
from jax.experimental.pallas import tpu as pltpu
from jax.sharding import PartitionSpec as P

MESH = pl.DeviceIdType.MESH
INNER = 4


def kernel(dp, tp, pieces, h_ref, w_ref, up_ref, gain_ref, normed_ref, gw_ref, gg_ref,
           h_all, w_all, stage, parts, merged, up_all, norm_buf, gmt, gstage, grecv,
           st, st_all, gg, gg_tp, gg_out, gg_in,
           local_sem, hs, hr, ws, wr, us, ur, rs_s, rs_r, st_s, st_r, ag_s, ag_r,
           ns, nr, gs, gr, g1s, g1r, g2s, g2r, g3s, g3r):
    outer = dp // INNER
    d, t = lax.axis_index("dp"), lax.axis_index("tp")
    o, i = d // INNER, d % INNER
    x, c = i // 2, i % 2
    tok = h_ref.shape[1]
    depth = h_ref.shape[2]
    chunks, chunk = w_all.shape[0], w_all.shape[1]
    per = chunks // outer
    rows = per * chunk
    draft = dp * rows
    half = tp // 2

    def inner_of(s):
        return ((x + s // 2) % 2) * 2 + (c + s % 2) % 2

    def near(s):
        return {"dp": o * INNER + inner_of(s)}

    def far(r):
        return {"dp": ((o + r) % outer) * INNER + i}

    def columns(block_o, block_i):
        return pl.ds(pl.multiple_of((block_o * INNER + block_i) * rows, 128), rows)

    def rdma(src, dst, ssem, rsem, dev):
        return pltpu.make_async_remote_copy(src_ref=src, dst_ref=dst, send_sem=ssem, recv_sem=rsem,
                                            device_id=dev, device_id_type=MESH)

    started = []

    def send(src, dst, ssem, rsem, dev):
        copy = rdma(src, dst, ssem, rsem, dev)
        copy.start()
        started.append(copy)

    mine = [pltpu.make_async_copy(h_ref, h_all.at[:, 0], local_sem.at[0]),
            pltpu.make_async_copy(w_ref, w_all.at[pl.ds(0, per)], local_sem.at[1])]
    for r in range(outer):
        mine.append(pltpu.make_async_copy(up_ref.at[:, columns((o + r) % outer, i)], up_all.at[0, r],
                                          local_sem.at[2 + r]))
    for copy in mine:
        copy.start()

    barrier = pltpu.get_barrier_semaphore()
    partners = ([near(s) for s in range(1, INNER)] + [far(r) for r in range(1, outer)]
                + [{"tp": (t + q) % tp} for q in range(1, tp)])
    for dev in partners:
        pl.semaphore_signal(barrier, inc=1, device_id=dev, device_id_type=MESH)
    pl.semaphore_wait(barrier, len(partners))

    def zpart(p):
        return pl.ds(p * (tp // pieces), tp // pieces)

    for p in range(pieces):
        send(h_ref.at[zpart(p)], h_all.at[zpart(p), 2], hs.at[0, p], hr.at[2, p], near(2))
    for r in range(1, outer):
        for j in range(per):
            slot = (outer - r) * per + j
            send(w_ref.at[j], w_all.at[slot], ws.at[slot], wr.at[slot], far(r))
    for p in range(pieces):
        send(h_ref.at[zpart(p)], h_all.at[zpart(p), 1], hs.at[1, p], hr.at[1, p], near(1))
    for s in range(1, INNER):
        for r in range(outer):
            send(up_ref.at[:, columns((o + r) % outer, inner_of(s))], up_all.at[s, r],
                 us.at[s, r], ur.at[s, r], near(s))

    def rs_copy(z, wc, s, src):
        return rdma(stage.at[wc, z, s], parts.at[src, wc, s], rs_s.at[z, wc, s],
                    rs_r.at[src, wc, s], {"tp": z})

    def product(z0, nz, s, wc):
        left = h_all[z0:z0 + nz, s].reshape(nz * tok, depth)
        out = lax.dot_general(left, w_all[wc], (((1,), (1,)), ((), ())),
                              preferred_element_type=jnp.float32)
        stage[wc, z0:z0 + nz, s] = out.astype(jnp.bfloat16).reshape(nz, tok, chunk)
        for z in range(z0, z0 + nz):
            @pl.when(t != z)
            def _():
                rs_copy(z, wc, s, t).start()

    def over(lo, hi, fn):
        def step(k, carry):
            fn(k)
            return carry
        lax.fori_loop(lo, hi, step, 0)

    mine[0].wait()
    mine[1].wait()
    over(0, per, lambda wc: product(0, tp, 0, wc))
    for p in range(pieces):
        rdma(h_ref.at[zpart(p)], h_all.at[zpart(p), 1], hs.at[1, p], hr.at[1, p], near(1)).wait_recv()
    over(0, per, lambda wc: product(0, tp, 1, wc))

    have_w, have_h = per, 0
    step_z = tp // pieces
    while have_w < chunks or have_h < pieces:
        if have_h < pieces:
            p = have_h
            rdma(h_ref.at[zpart(p)], h_all.at[zpart(p), 2], hs.at[0, p], hr.at[2, p], near(2)).wait_recv()
            send(h_all.at[zpart(p), 2], h_all.at[zpart(p), 3], hs.at[2, p], hr.at[3, p], near(1))
        if have_w < chunks:
            wc = have_w
            rdma(w_ref.at[0], w_all.at[wc], ws.at[wc], wr.at[wc], far(1)).wait_recv()
            over(0, 2, lambda s: product(0, tp, s, wc))
            for p in range(have_h):
                over(2, INNER, lambda s: product(p * step_z, step_z, s, wc))
            have_w += 1
        if have_h < pieces:
            p = have_h
            over(0, have_w, lambda wc: product(p * step_z, step_z, 2, wc))
            rdma(h_all.at[zpart(p), 2], h_all.at[zpart(p), 3], hs.at[2, p], hr.at[3, p], near(1)).wait_recv()
            over(0, have_w, lambda wc: product(p * step_z, step_z, 3, wc))
            have_h += 1

    for copy in mine[2:]:
        copy.wait()
    for s in range(1, INNER):
        for r in range(outer):
            rdma(up_ref.at[:, columns(o, i)], up_all.at[s, r], us.at[s, r], ur.at[s, r], near(s)).wait_recv()

    def gain_of(wc):
        r, j = wc // per, wc % per
        return gain_ref[(o + r) % outer, i, j]

    for s in range(INNER):
        sq = jnp.zeros((tok, 1), jnp.float32)
        al = jnp.zeros((tok, 1), jnp.float32)
        for wc in range(chunks):
            r, j = wc // per, wc % per
            total = stage[wc, t, s].astype(jnp.float32)
            for q in range(1, tp):
                src = (t + q) % tp
                rs_copy(t, wc, s, src).wait_recv()
                total = total + parts[src, wc, s].astype(jnp.float32)
            merged[s, wc] = total
            along = up_all[s, r, :, j * chunk:(j + 1) * chunk].astype(jnp.float32) * gain_of(wc)
            sq = sq + jnp.sum(total * total, axis=1, keepdims=True)
            al = al + jnp.sum(total * along, axis=1, keepdims=True)
        st[s:s + 1, :] = jnp.swapaxes(jnp.broadcast_to(sq, (tok, 128)), 0, 1)[0:1, :]
        st[INNER + s:INNER + s + 1, :] = jnp.swapaxes(jnp.broadcast_to(al, (tok, 128)), 0, 1)[0:1, :]
    for s in range(1, INNER):
        send(st, st_all.at[s], st_s.at[s], st_r.at[s], near(s))
    for s in range(1, INNER):
        rdma(st, st_all.at[s], st_s.at[s], st_r.at[s], near(s)).wait_recv()

    inverse, proj = [], []
    for s in range(INNER):
        sq, al = st[s:s + 1, :], st[INNER + s:INNER + s + 1, :]
        for q in range(1, INNER):
            k = ((s // 2 + q // 2) % 2) * 2 + (s + q) % 2
            sq = sq + st_all[q, k:k + 1, :]
            al = al + st_all[q, INNER + k:INNER + k + 1, :]
        inv = lax.rsqrt(sq / draft + 1e-05)
        pr = al * inv / draft
        inverse.append(jnp.swapaxes(jnp.broadcast_to(inv, (128, tok)), 0, 1)[:, 0:1])
        proj.append(jnp.swapaxes(jnp.broadcast_to(pr, (128, tok)), 0, 1)[:, 0:1])

    def ag_copy(wc, q, src):
        return rdma(gmt.at[wc, src], gmt.at[wc, src], ag_s.at[wc, q], ag_r.at[wc, src],
                    {"tp": (t + q) % tp})

    order = list(range(per, chunks)) + list(range(per))
    for wc in order:
        r, j = wc // per, wc % per
        gain = gain_of(wc)
        own = jnp.zeros((1, chunk), jnp.float32)
        for s in range(INNER):
            scaled = merged[s, wc] * inverse[s]
            incoming = up_all[s, r, :, j * chunk:(j + 1) * chunk].astype(jnp.float32)
            norm_buf[s, r, :, j * chunk:(j + 1) * chunk] = (scaled * gain).astype(jnp.bfloat16)
            own = own + jnp.sum(incoming * scaled, axis=0, keepdims=True)
            grad = inverse[s] * (incoming * gain - scaled * proj[s])
            gmt[wc, t, :, s * tok:(s + 1) * tok] = jnp.swapaxes(grad, 0, 1).astype(jnp.bfloat16)
        gg[wc:wc + 1, :] = own
        for q in range(1, tp):
            ag_copy(wc, q, t).start()

    for s in range(1, INNER):
        for r in range(outer):
            send(norm_buf.at[s, r], normed_ref.at[:, columns((o + r) % outer, i)],
                 ns.at[s, r], nr.at[s, r], near(s))
    keep = []
    for r in range(outer):
        copy = pltpu.make_async_copy(norm_buf.at[0, r], normed_ref.at[:, columns((o + r) % outer, i)],
                                     local_sem.at[2 + r])
        copy.start()
        keep.append(copy)
    for q in range(1, tp):
        send(gg, gg_tp.at[tp - q], g1s.at[q], g1r.at[tp - q], {"tp": (t + q) % tp})

    def gain_step(n):
        if n == 0:
            total = gg[...]
            for q in range(1, tp):
                rdma(gg, gg_tp.at[q], g1s.at[q], g1r.at[q], {"tp": (t + q) % tp}).wait_recv()
                total = total + gg_tp[q]
            gg_out[0] = total
            for r in range(1, outer):
                send(gg_out.at[0], gg_out.at[outer - r], g2s.at[r], g2r.at[outer - r], far(r))
        if n == 1:
            for r in range(1, outer):
                rdma(gg_out.at[0], gg_out.at[r], g2s.at[r], g2r.at[r], far(r)).wait_recv()
            for wc in range(chunks):
                total = gg_out[0, wc:wc + 1, :]
                for r in range(1, outer):
                    k = (wc - r * per) % chunks
                    total = total + gg_out[r, k:k + 1, :]
                gg_in[0, wc:wc + 1, :] = total
            for s in range(1, INNER):
                send(gg_in.at[0], gg_in.at[s], g3s.at[s], g3r.at[s], near(s))
        if n == 2:
            for s in range(1, INNER):
                rdma(gg_in.at[0], gg_in.at[s], g3s.at[s], g3r.at[s], near(s)).wait_recv()
            for s in range(INNER):
                for wc in range(chunks):
                    gg_ref[(o + wc // per) % outer, inner_of(s), wc % per] = gg_in[s, wc:wc + 1, :]

    tile = 512
    for n, wc in enumerate(order):
        for q in range(1, tp):
            ag_copy(wc, q, (t + q) % tp).wait_recv()

        def step(k, carry):
            cols = pl.ds(pl.multiple_of(k * tile, 128), tile)
            acc = jnp.zeros((chunk, tile), jnp.float32)
            for z in range(tp):
                right = h_all[z, :, :, cols].reshape(INNER * tok, tile)
                acc = acc + jnp.dot(gmt[wc, z], right, preferred_element_type=jnp.float32)
            if wc >= per:
                gstage[wc - per, :, cols] = acc.astype(jnp.bfloat16)
            else:
                gw_ref[wc, :, cols] = acc
            return carry
        lax.fori_loop(0, depth // tile, step, 0)
        if wc >= per:
            r, j = wc // per, wc % per
            slot = (outer - r - 1) * per + j
            send(gstage.at[wc - per], grecv.at[slot], gs.at[slot], gr.at[slot], far(r))
        gain_step(n)
    for j in range(per):
        for r in range(1, outer):
            slot = (r - 1) * per + j
            rdma(gstage.at[0], grecv.at[slot], gs.at[slot], gr.at[slot], far(r)).wait_recv()

        def add(k, carry):
            cols = pl.ds(pl.multiple_of(k * tile, 128), tile)
            total = gw_ref[j, :, cols]
            for r in range(1, outer):
                total = total + grecv[(r - 1) * per + j, :, cols].astype(jnp.float32)
            gw_ref[j, :, cols] = total
            return carry
        lax.fori_loop(0, depth // tile, add, 0)

    for s in range(1, INNER):
        for r in range(outer):
            rdma(norm_buf.at[s, r], normed_ref.at[:, columns((o + r) % outer, inner_of(s))],
                 ns.at[s, r], nr.at[s, r], near(s)).wait_recv()
    for copy in keep:
        copy.wait()
    for copy in started:
        copy.wait_send()
    for wc in range(chunks):
        for q in range(1, tp):
            ag_copy(wc, q, t).wait_send()
        for s in range(INNER):
            for q in range(1, tp):
                rs_copy((t + q) % tp, wc, s, t).wait_send()


def body(dp, tp, hidden_states, fc_weight, norm_gain, upstream, lengths):
    tok_group, layers, slab = hidden_states.shape
    rows = fc_weight.shape[0]
    tok, draft = upstream.shape
    depth = layers * slab
    outer = dp // INNER
    chunk = min(256, rows)
    per = rows // chunk
    chunks = outer * per
    pieces = 2 if tp % 2 == 0 else 1
    bf, f32 = jnp.bfloat16, jnp.float32
    pos = lax.broadcasted_iota(jnp.int32, (tok, 1), 0)
    incoming = upstream * (pos < lengths[0]).astype(bf)
    dma = pltpu.SemaphoreType.DMA
    hbm = pl.BlockSpec(memory_space=pl.ANY)
    vmem = pl.BlockSpec(memory_space=pltpu.VMEM)
    flops = 4 * tok_group * draft * depth
    normed, gw, gg = pl.pallas_call(
        functools.partial(kernel, dp, tp, pieces),
        out_shape=(jax.ShapeDtypeStruct((tok, draft), bf),
                   jax.ShapeDtypeStruct((per, chunk, depth), f32),
                   jax.ShapeDtypeStruct((outer, INNER, per, 1, chunk), f32)),
        in_specs=[hbm, hbm, hbm, vmem],
        out_specs=(hbm, vmem, vmem),
        scratch_shapes=[
            pltpu.VMEM((tp, INNER, tok, depth), bf),
            pltpu.VMEM((chunks, chunk, depth), bf),
            pltpu.VMEM((chunks, tp, INNER, tok, chunk), bf),
            pltpu.VMEM((tp, chunks, INNER, tok, chunk), bf),
            pltpu.VMEM((INNER, chunks, tok, chunk), f32),
            pltpu.VMEM((INNER, outer, tok, rows), bf),
            pltpu.VMEM((INNER, outer, tok, rows), bf),
            pltpu.VMEM((chunks, tp, chunk, INNER * tok), bf),
            pltpu.VMEM((max(1, chunks - per), chunk, depth), bf),
            pltpu.VMEM((max(1, chunks - per), chunk, depth), bf),
            pltpu.VMEM((2 * INNER, tok), f32),
            pltpu.VMEM((INNER, 2 * INNER, tok), f32),
            pltpu.VMEM((chunks, chunk), f32),
            pltpu.VMEM((tp, chunks, chunk), f32),
            pltpu.VMEM((outer, chunks, chunk), f32),
            pltpu.VMEM((INNER, chunks, chunk), f32),
            dma((2 + outer,)),
            dma((3, pieces)), dma((INNER, pieces)),
            dma((chunks,)), dma((chunks,)),
            dma((INNER, outer)), dma((INNER, outer)),
            dma((tp, chunks, INNER)), dma((tp, chunks, INNER)),
            dma((INNER,)), dma((INNER,)),
            dma((chunks, tp)), dma((chunks, tp)),
            dma((INNER, outer)), dma((INNER, outer)),
            dma((chunks,)), dma((chunks,)),
            dma((tp,)), dma((tp,)),
            dma((outer,)), dma((outer,)),
            dma((INNER,)), dma((INNER,)),
        ],
        compiler_params=pltpu.CompilerParams(collective_id=0, has_side_effects=True,
                                             vmem_limit_bytes=62 * 2**20),
        cost_estimate=pl.CostEstimate(flops=flops, bytes_accessed=8 * tok_group * depth,
                                      transcendentals=0),
    )(hidden_states.reshape(tp, tok, depth), fc_weight.reshape(per, chunk, depth), incoming,
      norm_gain.reshape(outer, INNER, per, 1, chunk))
    return normed, gw.reshape(rows, layers, slab), gg.reshape(draft)


def solution(mesh):
    return jax.shard_map(
        functools.partial(body, mesh.shape["dp"], mesh.shape["tp"]),
        mesh=mesh,
        in_specs=(
            P("dp", None, "tp"),
            P("dp", None, "tp"),
            P(),
            P(("dp", "tp"), None),
            P(("dp", "tp")),
        ),
        out_specs=(P(("dp", "tp"), None), P("dp", None, "tp"), P()),
        check_vma=False,
    )
```

time: 509 us -> 366 us (0.72)
  waiting for transfers between devices: 402 us -> 0 us
  Pallas kernels: 0 us -> 308 us
  local copies, waits for them, and re-layouts: 3.21 us -> 53.5 us
  blocking collectives: 38.9 us -> 0 us
  matrix products: 38.5 us -> 0 us
  between operations: 14.5 us -> 1.3 us
  other arithmetic: 11.2 us -> 2.34 us
    pallas_call x0 -> x1, Pallas kernels: none -> 308 us  [body(): pl.pallas_call(functools.partial(kernel, dp, tp, pieces), out_shape=(jax....]
    all_gather x2 -> x0, waiting for transfers between devices: 208 us -> none  [the longest x1 130 us: body(): weight_piece = lax.all_gather(fc_weight, 'dp', axis=0, tiled=True)]
    reduce_scatter x2 -> x0, waiting for transfers between devices: 193 us -> none  [the longest x1 117 us: body(): lax.psum_scatter(product.reshape(fc_weight.shape[0] * lax.axis_size('dp')...]
    reshape x0 -> x5, local copies, waits for them, and re-layouts: none -> 42.1 us  [the longest x2 16.4 us: body(): hidden_states.reshape(tp, tok, depth)]
    psum x1 -> x0, blocking collectives: 38.9 us -> none  [body(): grad_gain = lax.psum(jnp.sum(incoming * scaled, axis=0), ('dp', 'tp'))]
    dot_general x2 -> x0, matrix products: 38.5 us -> none  [the longest x1 19.3 us: body(): lax.dot_general(flat_hidden, flat_piece, contract_last, preferred_element...]
    unnamed x9, local copies, waits for them, and re-layouts: 3.21 us -> 11.4 us
    convert_element_type x3 -> x1, other arithmetic: 7.53 us -> 0.01 us  [body(): incoming = upstream * (pos < lengths[0]).astype(bf)]
  transfers between devices with their start and end apart: 4 -> 0, of which waited for: 4 -> 0; matrix products, arithmetic and copies ran while one was open for 1% -> 0% of each run, Pallas kernels for 0% -> 0%
where the time goes in v1:
time: 366 us; the launch traced here: 365 us
  Pallas kernels  308 us (84%)
  local copies, waits for them, and re-layouts  53.5 us (15%)
    pallas_call x1, Pallas kernels, body(): pl.pallas_call(functools.partial(kernel, dp, tp, pieces), out_shape=(jax....  308 us
    reshape x2, local copies, waits for them, and re-layouts, body(): hidden_states.reshape(tp, tok, depth)  16.4 us
    reshape x2, local copies, waits for them, and re-layouts, body(): fc_weight.reshape(per, chunk, depth)  14.3 us
    unnamed x9, local copies, waits for them, and re-layouts  11.4 us
    reshape x1, local copies, waits for them, and re-layouts, body(): return (normed, gw.reshape(rows, layers, slab), gg.reshape(draft))  11.3 us

profile of v1, /device:TPU:0, one launch (start us, length us, event | category | flops | bytes accessed | tf_op | source)
XLA Modules:
  0.0 364.7 jit_solution(3141226591585419984)
XLA Ops:
  1.3 2.3 broadcast_multiply_fusion.up_ref
  3.6 6.6 %copy.17 = bf16[512,3,1024]{2,1,0:T(4,128)(2,1)} copy(bf16[512,3,1024]{2,0,1:T(8,128)(2,1)} %param.5) | data formatting | bytes 6291456 | tf_op jit(solution)/shard_map/reshape | solution.py:346
  10.2 0.0 copy-start
  10.2 9.8 %reshape.33.h_ref = bf16[4,128,3072]{2,1,0:T(8,128)(2,1)} reshape(bf16[512,3,1024]{2,1,0:T(4,128)(2,1)} %copy.17) | data formatting | bytes 6291456 | tf_op jit(solution)/shard_map/reshape | solution.py:346
  20.0 0.0 copy-done
  20.0 4.7 %copy.18 = bf16[512,3,1024]{2,1,0:T(4,128)(2,1)} copy(bf16[512,3,1024]{2,0,1:T(8,128)(2,1)S(1)} %copy-done) | data formatting | bytes 6291456 | tf_op jit(solution)/shard_map/reshape | solution.py:346
  24.7 9.6 %reshape.34.w_ref = bf16[2,256,3072]{2,1,0:T(8,128)(2,1)} reshape(bf16[512,3,1024]{2,1,0:T(4,128)(2,1)} %copy.18) | data formatting | bytes 6291456 | tf_op jit(solution)/shard_map/reshape | solution.py:346
  34.4 307.6 %shard_map.76 = (bf16[128,4096]{1,0:T(8,128)(2,1)}, f32[2,256,3072]{2,1,0:T(8,128)}, f32[2,4,2,1,256]{4,3,2,1,0:T(1,128)}) custom-call(bf16[4,128,3072]{2,1,0:T(8,128)(2,1)} %reshape.33.h_ref, bf16[2,256,3072]{2,1,0:T(8,128)(2,1)} %reshape.34.w_ref, bf16[128,4096]{1,0:T(8,128)(2,1)} %broadcast_multiply_fusion.up_ref, f32[2,4,2,1,256]{4,3,2,1,0:T(1,128)} %bitcast.5), custom_call_target="tpu_custom_call" | custom-call | flops 25769803776 | bytes 12582912 | tf_op jit(solution)/shard_map/pallas_call | solution.py:305
  341.9 11.3 %reshape.35 = f32[512,3,1024]{2,1,0:T(4,128)} reshape(f32[2,256,3072]{2,1,0:T(8,128)} %get-tuple-element.7) | data formatting | bytes 12582912 | tf_op jit(solution)/shard_map/reshape | solution.py:348
  353.3 0.0 copy-start.1
  353.3 0.0 copy-start.2
  353.3 9.8 %copy.16 = f32[512,3,1024]{2,0,1:T(8,128)} copy(f32[512,3,1024]{2,1,0:T(4,128)} %reshape.35) | data formatting | bytes 12582912
  363.1 0.0 copy-done.1
  363.1 1.0 copy.26
  364.1 0.0 copy-done.2
  364.1 0.6 copy.27
  (1 shorter events, 0.0 us)
Async XLA Ops:
  10.2 9.8 %copy-start = (bf16[512,3,1024]{2,0,1:T(8,128)(2,1)S(1)}, bf16[512,3,1024]{2,0,1:T(8,128)(2,1)}, u32[]{:S(2)}) copy-start(bf16[512,3,1024]{2,0,1:T(8,128)(2,1)} %param.6) | copy-start | bytes 9437188
  353.3 9.8 %copy-start.1 = (bf16[128,4096]{1,0:T(8,128)(2,1)S(1)}, bf16[128,4096]{1,0:T(8,128)(2,1)}, u32[]{:S(2)}) copy-start(bf16[128,4096]{1,0:T(8,128)(2,1)} %get-tuple-element.18) | copy-start | bytes 3145732
  353.3 10.8 %copy-start.2 = (f32[2,4,2,1,256]{4,3,2,1,0:T(1,128)S(1)}, f32[2,4,2,1,256]{4,3,2,1,0:T(1,128)}, u32[]{:S(2)}) copy-start(f32[2,4,2,1,256]{4,3,2,1,0:T(1,128)} %get-tuple-element.8) | copy-start | bytes 49156

commit v2 on v1

v2 whole, which is shorter than its diff:
```python
import functools

import jax
import jax.numpy as jnp
from jax import lax
from jax.experimental import pallas as pl
from jax.experimental.pallas import tpu as pltpu
from jax.sharding import PartitionSpec as P

MESH = pl.DeviceIdType.MESH
INNER = 4


def kernel(dp, tp, h_ref, w_ref, up_ref, gain_ref, normed_ref, gw_ref, gg_ref,
           h_all, w_all, stage, parts, merged, up_all, norm_buf, gmt, gstage, grecv,
           st, st_all, gg, gg_tp, gg_out, gg_in,
           local_sem, hs, hr, ws, wr, us, ur, rs_s, rs_r, st_s, st_r, ag_s, ag_r,
           ns, nr, gs, gr, g1s, g1r, g2s, g2r, g3s, g3r):
    outer = dp // INNER
    d, t = lax.axis_index("dp"), lax.axis_index("tp")
    o, i = d // INNER, d % INNER
    x, c = i // 2, i % 2
    layers, _, tok, slab = h_ref.shape
    chunks, chunk = w_all.shape[1], w_all.shape[2]
    per = chunks // outer
    rows = per * chunk
    draft = dp * rows

    def inner_of(s):
        return ((x + s // 2) % 2) * 2 + (c + s % 2) % 2

    def near(s):
        return {"dp": o * INNER + inner_of(s)}

    def far(r):
        return {"dp": ((o + r) % outer) * INNER + i}

    def columns(block_o, block_i):
        return pl.ds(pl.multiple_of((block_o * INNER + block_i) * rows, 128), rows)

    def rdma(src, dst, ssem, rsem, dev):
        return pltpu.make_async_remote_copy(src_ref=src, dst_ref=dst, send_sem=ssem, recv_sem=rsem,
                                            device_id=dev, device_id_type=MESH)

    started = []

    def send(src, dst, ssem, rsem, dev):
        copy = rdma(src, dst, ssem, rsem, dev)
        copy.start()
        started.append(copy)

    mine = [pltpu.make_async_copy(h_ref, h_all.at[:, :, 0], local_sem.at[0]),
            pltpu.make_async_copy(w_ref, w_all.at[:, pl.ds(0, per)], local_sem.at[1])]
    for r in range(outer):
        mine.append(pltpu.make_async_copy(up_ref.at[:, columns((o + r) % outer, i)], up_all.at[0, r],
                                          local_sem.at[2 + r]))
    for copy in mine:
        copy.start()

    barrier = pltpu.get_barrier_semaphore()
    partners = ([near(s) for s in range(1, INNER)] + [far(r) for r in range(1, outer)]
                + [{"tp": (t + q) % tp} for q in range(1, tp)])
    for dev in partners:
        pl.semaphore_signal(barrier, inc=1, device_id=dev, device_id_type=MESH)
    pl.semaphore_wait(barrier, len(partners))

    def h_copy(p):
        return rdma(h_ref.at[:, p], h_all.at[:, p, 2], hs.at[0, p], hr.at[2, p], near(2))

    def own_copy(p):
        return rdma(h_ref.at[:, p], h_all.at[:, p, 1], hs.at[1, p], hr.at[1, p], near(1))

    def pass_copy(p):
        return rdma(h_all.at[:, p, 2], h_all.at[:, p, 3], hs.at[2, p], hr.at[3, p], near(1))

    def w_copy(m):
        wc, l = per + m // layers, m % layers
        r, j = outer - wc // per, wc % per
        return rdma(w_ref.at[l, j], w_all.at[l, wc], ws.at[m], wr.at[m], far(r))

    def go(copy):
        copy.start()
        started.append(copy)

    n_w = (chunks - per) * layers
    for p in range(min(2, tp)):
        go(h_copy(p))
    for m in range(min(2, n_w)):
        go(w_copy(m))
    for p in range(tp):
        go(own_copy(p))

    def rs_copy(z, wc, a, src):
        pair = pl.ds(2 * a, 2)
        return rdma(stage.at[wc, z, pair], parts.at[src, wc, pair], rs_s.at[z, wc, a],
                    rs_r.at[src, wc, a], {"tp": z})

    def product(z, a, wc):
        out = jnp.zeros((2 * tok, chunk), jnp.float32)
        for l in range(layers):
            left = h_all[l, z, 2 * a:2 * a + 2].reshape(2 * tok, slab)
            out = out + lax.dot_general(left, w_all[l, wc], (((1,), (1,)), ((), ())),
                                        preferred_element_type=jnp.float32)
        stage[wc, z, 2 * a:2 * a + 2] = out.astype(jnp.bfloat16).reshape(2, tok, chunk)

        @pl.when(t != z)
        def _():
            rs_copy(z, wc, a, t).start()

    def over(lo, hi, fn):
        def step(k, carry):
            fn(k)
            return carry
        lax.fori_loop(lo, hi, step, 0)

    mine[0].wait()
    mine[1].wait()
    for p in range(tp):
        own_copy(p).wait_recv()
    for wc in range(per):
        over(0, tp, lambda z: product((t + 1 + z) % tp, 0, wc))

    events = sorted([((p + 1) / tp, 1, p) for p in range(tp)]
                    + [((m + 1) / n_w, 0, m) for m in range(n_w)])
    have_w, have_h = per, 0
    for _, kind, n in events:
        if kind == 0:
            w_copy(n).wait_recv()
            if n + 2 < n_w:
                go(w_copy(n + 2))
            if n % layers == layers - 1:
                wc = have_w
                over(0, tp, lambda z: product((t + 1 + z) % tp, 0, wc))
                over(0, have_h, lambda z: product(z, 1, wc))
                have_w += 1
        else:
            h_copy(n).wait_recv()
            go(pass_copy(n))
            if n + 2 < tp:
                go(h_copy(n + 2))
            pass_copy(n).wait_recv()
            over(0, have_w, lambda wc: product(n, 1, wc))
            have_h += 1
            if have_h == tp:
                for s in range(1, INNER):
                    for r in range(outer):
                        send(up_ref.at[:, columns((o + r) % outer, inner_of(s))], up_all.at[s, r],
                             us.at[s, r], ur.at[s, r], near(s))

    for copy in mine[2:]:
        copy.wait()
    for s in range(1, INNER):
        for r in range(outer):
            rdma(up_ref.at[:, columns(o, i)], up_all.at[s, r], us.at[s, r], ur.at[s, r], near(s)).wait_recv()

    def gain_of(wc):
        r, j = wc // per, wc % per
        return gain_ref[(o + r) % outer, i, j]

    for s in range(INNER):
        sq = jnp.zeros((tok, 1), jnp.float32)
        al = jnp.zeros((tok, 1), jnp.float32)
        for wc in range(chunks):
            r, j = wc // per, wc % per
            total = stage[wc, t, s].astype(jnp.float32)
            for q in range(1, tp):
                src = (t + q) % tp
                if s % 2 == 0:
                    rs_copy(t, wc, s // 2, src).wait_recv()
                total = total + parts[src, wc, s].astype(jnp.float32)
            merged[s, wc] = total
            along = up_all[s, r, :, j * chunk:(j + 1) * chunk].astype(jnp.float32) * gain_of(wc)
            sq = sq + jnp.sum(total * total, axis=1, keepdims=True)
            al = al + jnp.sum(total * along, axis=1, keepdims=True)
        st[s:s + 1, :] = jnp.swapaxes(jnp.broadcast_to(sq, (tok, 128)), 0, 1)[0:1, :]
        st[INNER + s:INNER + s + 1, :] = jnp.swapaxes(jnp.broadcast_to(al, (tok, 128)), 0, 1)[0:1, :]
    for s in range(1, INNER):
        send(st, st_all.at[s], st_s.at[s], st_r.at[s], near(s))
    for s in range(1, INNER):
        rdma(st, st_all.at[s], st_s.at[s], st_r.at[s], near(s)).wait_recv()

    inverse, proj = [], []
    for s in range(INNER):
        sq, al = st[s:s + 1, :], st[INNER + s:INNER + s + 1, :]
        for q in range(1, INNER):
            k = ((s // 2 + q // 2) % 2) * 2 + (s + q) % 2
            sq = sq + st_all[q, k:k + 1, :]
            al = al + st_all[q, INNER + k:INNER + k + 1, :]
        inv = lax.rsqrt(sq / draft + 1e-05)
        pr = al * inv / draft
        inverse.append(jnp.swapaxes(jnp.broadcast_to(inv, (128, tok)), 0, 1)[:, 0:1])
        proj.append(jnp.swapaxes(jnp.broadcast_to(pr, (128, tok)), 0, 1)[:, 0:1])

    def ag_copy(wc, src, dr):
        side = (dr + 1) // 2
        return rdma(gmt.at[wc, src], gmt.at[wc, src], ag_s.at[wc, side, src],
                    ag_r.at[wc, side, src], {"tp": (t + dr + tp) % tp})

    def ag_own(wc):
        @pl.when(t < tp - 1)
        def _():
            ag_copy(wc, t, 1).start()

        @pl.when(t > 0)
        def _():
            ag_copy(wc, t, -1).start()

    def ag_take(wc):
        for k in range(1, tp):
            @pl.when(t - k >= 0)
            def _():
                ag_copy(wc, (t - k + tp) % tp, 1).wait_recv()

                @pl.when(t < tp - 1)
                def _():
                    ag_copy(wc, (t - k + tp) % tp, 1).start()

            @pl.when(t + k < tp)
            def _():
                ag_copy(wc, (t + k) % tp, -1).wait_recv()

                @pl.when(t > 0)
                def _():
                    ag_copy(wc, (t + k) % tp, -1).start()

    def ag_done(wc):
        for k in range(tp):
            @pl.when((t - k >= 0) & (t < tp - 1))
            def _():
                ag_copy(wc, (t - k + tp) % tp, 1).wait_send()

            @pl.when((t + k < tp) & (t > 0))
            def _():
                ag_copy(wc, (t + k) % tp, -1).wait_send()

    order = list(range(per, chunks)) + list(range(per))
    for wc in order:
        r, j = wc // per, wc % per
        gain = gain_of(wc)
        own = jnp.zeros((1, chunk), jnp.float32)
        for s in range(INNER):
            scaled = merged[s, wc] * inverse[s]
            incoming = up_all[s, r, :, j * chunk:(j + 1) * chunk].astype(jnp.float32)
            norm_buf[s, r, :, j * chunk:(j + 1) * chunk] = (scaled * gain).astype(jnp.bfloat16)
            own = own + jnp.sum(incoming * scaled, axis=0, keepdims=True)
            grad = inverse[s] * (incoming * gain - scaled * proj[s])
            gmt[wc, t, :, s * tok:(s + 1) * tok] = jnp.swapaxes(grad, 0, 1).astype(jnp.bfloat16)
        gg[wc:wc + 1, :] = own
        if wc in order[:2]:
            ag_own(wc)

    for s in range(1, INNER):
        for r in range(outer):
            send(norm_buf.at[s, r], normed_ref.at[:, columns((o + r) % outer, i)],
                 ns.at[s, r], nr.at[s, r], near(s))
    keep = []
    for r in range(outer):
        copy = pltpu.make_async_copy(norm_buf.at[0, r], normed_ref.at[:, columns((o + r) % outer, i)],
                                     local_sem.at[2 + r])
        copy.start()
        keep.append(copy)
    for q in range(1, tp):
        send(gg, gg_tp.at[tp - q], g1s.at[q], g1r.at[tp - q], {"tp": (t + q) % tp})

    def gain_step(n):
        if n == 0:
            total = gg[...]
            for q in range(1, tp):
                rdma(gg, gg_tp.at[q], g1s.at[q], g1r.at[q], {"tp": (t + q) % tp}).wait_recv()
                total = total + gg_tp[q]
            gg_out[0] = total
            for r in range(1, outer):
                send(gg_out.at[0], gg_out.at[outer - r], g2s.at[r], g2r.at[outer - r], far(r))
        if n == 1:
            for r in range(1, outer):
                rdma(gg_out.at[0], gg_out.at[r], g2s.at[r], g2r.at[r], far(r)).wait_recv()
            for wc in range(chunks):
                total = gg_out[0, wc:wc + 1, :]
                for r in range(1, outer):
                    k = (wc - r * per) % chunks
                    total = total + gg_out[r, k:k + 1, :]
                gg_in[0, wc:wc + 1, :] = total
            for s in range(1, INNER):
                send(gg_in.at[0], gg_in.at[s], g3s.at[s], g3r.at[s], near(s))
        if n == 2:
            for s in range(1, INNER):
                rdma(gg_in.at[0], gg_in.at[s], g3s.at[s], g3r.at[s], near(s)).wait_recv()
            for s in range(INNER):
                for wc in range(chunks):
                    gg_ref[(o + wc // per) % outer, inner_of(s), wc % per] = gg_in[s, wc:wc + 1, :]

    tile = min(512, slab)

    def g_copy(k, l, r):
        slot = (outer - r - 1) * per + k % per
        return rdma(gstage.at[k, l], grecv.at[slot, l], gs.at[slot, l], gr.at[slot, l], far(r))

    for n, wc in enumerate(order):
        ag_take(wc)
        if n + 2 < chunks:
            ag_own(order[n + 2])
        for l in range(layers):
            def step(k, carry):
                cols = pl.ds(pl.multiple_of(k * tile, 128), tile)
                acc = jnp.zeros((chunk, tile), jnp.float32)
                for z in range(tp):
                    right = h_all[l, z, :, :, cols].reshape(INNER * tok, tile)
                    acc = acc + jnp.dot(gmt[wc, z], right, preferred_element_type=jnp.float32)
                if wc >= per:
                    gstage[wc - per, l, :, cols] = acc.astype(jnp.bfloat16)
                else:
                    gw_ref[l, wc, :, cols] = acc
                return carry
            lax.fori_loop(0, slab // tile, step, 0)
            if wc >= per:
                go(g_copy(wc - per, l, wc // per))
        gain_step(n)
    for j in range(per):
        for l in range(layers):
            for r in range(1, outer):
                slot = (r - 1) * per + j
                rdma(gstage.at[0, l], grecv.at[slot, l], gs.at[slot, l], gr.at[slot, l], far(r)).wait_recv()

            def add(k, carry):
                cols = pl.ds(pl.multiple_of(k * tile, 128), tile)
                total = gw_ref[l, j, :, cols]
                for r in range(1, outer):
                    total = total + grecv[(r - 1) * per + j, l, :, cols].astype(jnp.float32)
                gw_ref[l, j, :, cols] = total
                return carry
            lax.fori_loop(0, slab // tile, add, 0)

    for s in range(1, INNER):
        for r in range(outer):
            rdma(norm_buf.at[s, r], normed_ref.at[:, columns((o + r) % outer, inner_of(s))],
                 ns.at[s, r], nr.at[s, r], near(s)).wait_recv()
    for copy in keep:
        copy.wait()
    for copy in started:
        copy.wait_send()
    for wc in range(chunks):
        ag_done(wc)
        for a in range(INNER // 2):
            for q in range(1, tp):
                rs_copy((t + q) % tp, wc, a, t).wait_send()


def body(dp, tp, hidden_states, fc_weight, norm_gain, upstream, lengths):
    tok_group, layers, slab = hidden_states.shape
    rows = fc_weight.shape[0]
    tok, draft = upstream.shape
    depth = layers * slab
    outer = dp // INNER
    chunk = min(256, rows)
    per = rows // chunk
    chunks = outer * per
    bf, f32 = jnp.bfloat16, jnp.float32
    pos = lax.broadcasted_iota(jnp.int32, (tok, 1), 0)
    incoming = upstream * (pos < lengths[0]).astype(bf)
    dma = pltpu.SemaphoreType.DMA
    hbm = pl.BlockSpec(memory_space=pl.ANY)
    vmem = pl.BlockSpec(memory_space=pltpu.VMEM)
    flops = 4 * tok_group * draft * depth
    normed, gw, gg = pl.pallas_call(
        functools.partial(kernel, dp, tp),
        out_shape=(jax.ShapeDtypeStruct((tok, draft), bf),
                   jax.ShapeDtypeStruct((layers, per, chunk, slab), f32),
                   jax.ShapeDtypeStruct((outer, INNER, per, 1, chunk), f32)),
        in_specs=[hbm, hbm, hbm, vmem],
        out_specs=(hbm, vmem, vmem),
        scratch_shapes=[
            pltpu.VMEM((layers, tp, INNER, tok, slab), bf),
            pltpu.VMEM((layers, chunks, chunk, slab), bf),
            pltpu.VMEM((chunks, tp, INNER, tok, chunk), bf),
            pltpu.VMEM((tp, chunks, INNER, tok, chunk), bf),
            pltpu.VMEM((INNER, chunks, tok, chunk), f32),
            pltpu.VMEM((INNER, outer, tok, rows), bf),
            pltpu.VMEM((INNER, outer, tok, rows), bf),
            pltpu.VMEM((chunks, tp, chunk, INNER * tok), bf),
            pltpu.VMEM((max(1, chunks - per), layers, chunk, slab), bf),
            pltpu.VMEM((max(1, chunks - per), layers, chunk, slab), bf),
            pltpu.VMEM((2 * INNER, tok), f32),
            pltpu.VMEM((INNER, 2 * INNER, tok), f32),
            pltpu.VMEM((chunks, chunk), f32),
            pltpu.VMEM((tp, chunks, chunk), f32),
            pltpu.VMEM((outer, chunks, chunk), f32),
            pltpu.VMEM((INNER, chunks, chunk), f32),
            dma((2 + outer,)),
            dma((3, tp)), dma((INNER, tp)),
            dma((chunks * layers,)), dma((chunks * layers,)),
            dma((INNER, outer)), dma((INNER, outer)),
            dma((tp, chunks, INNER // 2)), dma((tp, chunks, INNER // 2)),
            dma((INNER,)), dma((INNER,)),
            dma((chunks, 2, tp)), dma((chunks, 2, tp)),
            dma((INNER, outer)), dma((INNER, outer)),
            dma((chunks, layers)), dma((chunks, layers)),
            dma((tp,)), dma((tp,)),
            dma((outer,)), dma((outer,)),
            dma((INNER,)), dma((INNER,)),
        ],
        compiler_params=pltpu.CompilerParams(collective_id=0, has_side_effects=True,
                                             vmem_limit_bytes=62 * 2**20),
        cost_estimate=pl.CostEstimate(flops=flops, bytes_accessed=8 * tok_group * depth,
                                      transcendentals=0),
    )(hidden_states.transpose(1, 0, 2).reshape(layers, tp, tok, slab),
      fc_weight.transpose(1, 0, 2).reshape(layers, per, chunk, slab), incoming,
      norm_gain.reshape(outer, INNER, per, 1, chunk))
    return normed, gw.reshape(layers, rows, slab).transpose(1, 0, 2), gg.reshape(draft)


def solution(mesh):
    return jax.shard_map(
        functools.partial(body, mesh.shape["dp"], mesh.shape["tp"]),
        mesh=mesh,
        in_specs=(
            P("dp", None, "tp"),
            P("dp", None, "tp"),
            P(),
            P(("dp", "tp"), None),
            P(("dp", "tp")),
        ),
        out_specs=(P(("dp", "tp"), None), P("dp", None, "tp"), P()),
        check_vma=False,
    )
```

time: 366 us -> 232 us (0.63)
  Pallas kernels: 308 us -> 218 us
  local copies, waits for them, and re-layouts: 53.5 us -> 9.52 us
    pallas_call x1, Pallas kernels: 308 us -> 218 us  [body(): pl.pallas_call(functools.partial(kernel, dp, tp), out_shape=(jax.ShapeDty...]
    reshape x5 -> x0, local copies, waits for them, and re-layouts: 42.1 us -> none  [the longest x2 16.4 us: body(): hidden_states.reshape(tp, tok, depth)]
    unnamed x9 -> x5, local copies, waits for them, and re-layouts: 11.4 us -> 9.52 us
where the time goes in v2:
time: 232 us; the launch traced here: 231 us
  Pallas kernels  218 us (94%)
  local copies, waits for them, and re-layouts  9.52 us (4%)
  other arithmetic  2.34 us (1%)
    pallas_call x1, Pallas kernels, body(): pl.pallas_call(functools.partial(kernel, dp, tp), out_shape=(jax.ShapeDty...  218 us
    unnamed x5, local copies, waits for them, and re-layouts  9.52 us

profile of v2, /device:TPU:0, one launch (start us, length us, event | category | flops | bytes accessed | tf_op | source)
XLA Modules:
  0.0 231.4 jit_solution(12175905965715904492)
XLA Ops:
  1.3 2.3 %broadcast_multiply_fusion.up_ref = bf16[128,4096]{1,0:T(8,128)(2,1)} fusion(bf16[128,4096]{1,0:T(8,128)(2,1)} %param.8, bf16[128]{0:T(256)(128)(2,1)S(1)} %compare_convert_fusion), kind=kLoop, calls=%fused_computation | loop fusion | flops 524288 | bytes 2097408 | tf_op jit(solution)/shard_map/mul | solution.py:359
  3.6 218.3 %shard_map.76 = (bf16[128,4096]{1,0:T(8,128)(2,1)}, f32[3,2,256,1024]{3,2,1,0:T(8,128)}, f32[2,4,2,1,256]{4,3,2,1,0:T(1,128)}) custom-call(bf16[3,4,128,1024]{3,2,1,0:T(8,128)(2,1)} %bitcast.15, bf16[3,2,256,1024]{3,2,1,0:T(8,128)(2,1)} %bitcast.16, bf16[128,4096]{1,0:T(8,128)(2,1)} %broadcast_multiply_fusion.up_ref, f32[2,4,2,1,256]{4,3,2,1,0:T(1,128)} %bitcast.17), custom_call_target="tpu_custom_call" | custom-call | flops 25769803776 | bytes 12582912 | tf_op jit(solution)/shard_map/pallas_call | solution.py:364
  221.9 2.3 copy.12
  224.2 0.0 copy-start
  224.2 6.6 %copy.13 = f32[512,3,1024]{2,0,1:T(8,128)} copy(f32[512,3,1024]{2,0,1:T(8,128)} %bitcast.13) | data formatting | bytes 12582912
  230.8 0.0 copy-done
  230.8 0.6 copy.14
  (1 shorter events, 0.0 us)
Async XLA Ops:
  224.2 6.6 %copy-start = (f32[2,4,2,1,256]{4,3,2,1,0:T(1,128)S(1)}, f32[2,4,2,1,256]{4,3,2,1,0:T(1,128)}, u32[]{:S(2)}) copy-start(f32[2,4,2,1,256]{4,3,2,1,0:T(1,128)} %get-tuple-element.8) | copy-start | bytes 49156

commit v3 on v2

--- a/solution.py
+++ b/solution.py
@@ -11,11 +11,11 @@
 INNER = 4
 
 
-def kernel(dp, tp, h_ref, w_ref, up_ref, gain_ref, normed_ref, gw_ref, gg_ref,
-           h_all, w_all, stage, parts, merged, up_all, norm_buf, gmt, gstage, grecv,
+def kernel(dp, tp, h_ref, w_ref, up_ref, gain_ref, len_ref, normed_ref, gown_ref, grecv, gg_ref,
+           h_all, w_all, stage, parts, merged, up_all, norm_buf, gmt, gstage, gown, up_v,
            st, st_all, gg, gg_tp, gg_out, gg_in,
            local_sem, hs, hr, ws, wr, us, ur, rs_s, rs_r, st_s, st_r, ag_s, ag_r,
-           ns, nr, gs, gr, g1s, g1r, g2s, g2r, g3s, g3r):
+           ns, nr, gs, gr, go_s, g1s, g1r, g2s, g2r, g3s, g3r):
     outer = dp // INNER
     d, t = lax.axis_index("dp"), lax.axis_index("tp")
     o, i = d // INNER, d % INNER
@@ -24,6 +24,10 @@
     chunks, chunk = w_all.shape[1], w_all.shape[2]
     per = chunks // outer
     rows = per * chunk
+    part = gmt.shape[2]
+    split = chunk // part
+    per_g = per * split
+    parts_g = chunks * split
     draft = dp * rows
 
     def inner_of(s):
@@ -51,9 +55,7 @@
 
     mine = [pltpu.make_async_copy(h_ref, h_all.at[:, :, 0], local_sem.at[0]),
             pltpu.make_async_copy(w_ref, w_all.at[:, pl.ds(0, per)], local_sem.at[1])]
-    for r in range(outer):
-        mine.append(pltpu.make_async_copy(up_ref.at[:, columns((o + r) % outer, i)], up_all.at[0, r],
-                                          local_sem.at[2 + r]))
+    mine.append(pltpu.make_async_copy(up_ref, up_v, local_sem.at[2]))
     for copy in mine:
         copy.start()
 
@@ -115,10 +117,21 @@
 
     mine[0].wait()
     mine[1].wait()
+    mine[2].wait()
+    live = (lax.broadcasted_iota(jnp.int32, (tok, 1), 0) < len_ref[0]).astype(jnp.float32)
     for p in range(tp):
         own_copy(p).wait_recv()
     for wc in range(per):
         over(0, tp, lambda z: product((t + 1 + z) % tp, 0, wc))
+
+    def mask(k):
+        cols = pl.ds(pl.multiple_of(k * rows, 128), rows)
+        up_v[:, cols] = (up_v[:, cols].astype(jnp.float32) * live).astype(jnp.bfloat16)
+    over(0, dp, mask)
+    local = [pltpu.make_async_copy(up_v.at[:, columns((o + r) % outer, i)], up_all.at[0, r],
+                                   local_sem.at[2 + r]) for r in range(outer)]
+    for copy in local:
+        copy.start()
 
     events = sorted([((p + 1) / tp, 1, p) for p in range(tp)]
                     + [((m + 1) / n_w, 0, m) for m in range(n_w)])
@@ -144,14 +157,14 @@
             if have_h == tp:
                 for s in range(1, INNER):
                     for r in range(outer):
-                        send(up_ref.at[:, columns((o + r) % outer, inner_of(s))], up_all.at[s, r],
+                        send(up_v.at[:, columns((o + r) % outer, inner_of(s))], up_all.at[s, r],
                              us.at[s, r], ur.at[s, r], near(s))
 
-    for copy in mine[2:]:
+    for copy in local:
         copy.wait()
     for s in range(1, INNER):
         for r in range(outer):
-            rdma(up_ref.at[:, columns(o, i)], up_all.at[s, r], us.at[s, r], ur.at[s, r], near(s)).wait_recv()
+            rdma(up_v.at[:, columns(o, i)], up_all.at[s, r], us.at[s, r], ur.at[s, r], near(s)).wait_recv()
 
     def gain_of(wc):
         r, j = wc // per, wc % per
@@ -233,21 +246,23 @@
             def _():
                 ag_copy(wc, (t + k) % tp, -1).wait_send()
 
-    order = list(range(per, chunks)) + list(range(per))
-    for wc in order:
-        r, j = wc // per, wc % per
-        gain = gain_of(wc)
-        own = jnp.zeros((1, chunk), jnp.float32)
+    order = list(range(per_g, parts_g)) + list(range(per_g))
+    for g in order:
+        r, j, wc = g // per_g, g % per_g, g // split
+        here = slice(j * part, (j + 1) * part)
+        sub = slice((g % split) * part, (g % split + 1) * part)
+        gain = gain_of(wc)[:, sub]
+        own = jnp.zeros((1, part), jnp.float32)
         for s in range(INNER):
-            scaled = merged[s, wc] * inverse[s]
-            incoming = up_all[s, r, :, j * chunk:(j + 1) * chunk].astype(jnp.float32)
-            norm_buf[s, r, :, j * chunk:(j + 1) * chunk] = (scaled * gain).astype(jnp.bfloat16)
+            scaled = merged[s, wc, :, sub] * inverse[s]
+            incoming = up_all[s, r, :, here].astype(jnp.float32)
+            norm_buf[s, r, :, here] = (scaled * gain).astype(jnp.bfloat16)
             own = own + jnp.sum(incoming * scaled, axis=0, keepdims=True)
             grad = inverse[s] * (incoming * gain - scaled * proj[s])
-            gmt[wc, t, :, s * tok:(s + 1) * tok] = jnp.swapaxes(grad, 0, 1).astype(jnp.bfloat16)
-        gg[wc:wc + 1, :] = own
-        if wc in order[:2]:
-            ag_own(wc)
+            gmt[g, t, :, s * tok:(s + 1) * tok] = jnp.swapaxes(grad, 0, 1).astype(jnp.bfloat16)
+        gg[wc:wc + 1, sub] = own
+        if g in order[:2]:
+            ag_own(g)
 
     for s in range(1, INNER):
         for r in range(outer):
@@ -292,43 +307,38 @@
     tile = min(512, slab)
 
     def g_copy(k, l, r):
-        slot = (outer - r - 1) * per + k % per
-        return rdma(gstage.at[k, l], grecv.at[slot, l], gs.at[slot, l], gr.at[slot, l], far(r))
-
-    for n, wc in enumerate(order):
-        ag_take(wc)
-        if n + 2 < chunks:
+        return rdma(gstage.at[k, l], grecv.at[outer - r - 1, l, k % per_g], gs.at[k, l],
+                    gr.at[outer - r - 1, l, k % per_g], far(r))
+
+    for n, g in enumerate(order):
+        ag_take(g)
+        if n + 2 < parts_g:
             ag_own(order[n + 2])
         for l in range(layers):
             def step(k, carry):
                 cols = pl.ds(pl.multiple_of(k * tile, 128), tile)
-                acc = jnp.zeros((chunk, tile), jnp.float32)
+                acc = jnp.zeros((part, tile), jnp.float32)
                 for z in range(tp):
                     right = h_all[l, z, :, :, cols].reshape(INNER * tok, tile)
-                    acc = acc + jnp.dot(gmt[wc, z], right, preferred_element_type=jnp.float32)
-                if wc >= per:
-                    gstage[wc - per, l, :, cols] = acc.astype(jnp.bfloat16)
+                    acc = acc + jnp.dot(gmt[g, z], right, preferred_element_type=jnp.float32)
+                if g >= per_g:
+                    gstage[g - per_g, l, :, cols] = acc.astype(jnp.bfloat16)
                 else:
-                    gw_ref[l, wc, :, cols] = acc
+                    gown[l, g, :, cols] = acc.astype(jnp.bfloat16)
                 return carry
             lax.fori_loop(0, slab // tile, step, 0)
-            if wc >= per:
-                go(g_copy(wc - per, l, wc // per))
-        gain_step(n)
-    for j in range(per):
-        for l in range(layers):
-            for r in range(1, outer):
-                slot = (r - 1) * per + j
-                rdma(gstage.at[0, l], grecv.at[slot, l], gs.at[slot, l], gr.at[slot, l], far(r)).wait_recv()
-
-            def add(k, carry):
-                cols = pl.ds(pl.multiple_of(k * tile, 128), tile)
-                total = gw_ref[l, j, :, cols]
-                for r in range(1, outer):
-                    total = total + grecv[(r - 1) * per + j, l, :, cols].astype(jnp.float32)
-                gw_ref[l, j, :, cols] = total
-                return carry
-            lax.fori_loop(0, slab // tile, add, 0)
+            if g >= per_g:
+                go(g_copy(g - per_g, l, g // per_g))
+            else:
+                copy = pltpu.make_async_copy(gown.at[l, g], gown_ref.at[l, g], go_s.at[l, g])
+                copy.start()
+                keep.append(copy)
+        if n % 2 == 1:
+            gain_step(n // 2)
+    for r in range(1, outer):
+        for j in range(per_g):
+            for l in range(layers):
+                rdma(gstage.at[0, l], grecv.at[r - 1, l, j], gs.at[j, l], gr.at[r - 1, l, j], far(r)).wait_recv()
 
     for s in range(1, INNER):
         for r in range(outer):
@@ -338,8 +348,9 @@
         copy.wait()
     for copy in started:
         copy.wait_send()
+    for g in range(parts_g):
+        ag_done(g)
     for wc in range(chunks):
-        ag_done(wc)
         for a in range(INNER // 2):
             for q in range(1, tp):
                 rs_copy((t + q) % tp, wc, a, t).wait_send()
@@ -355,19 +366,20 @@
     per = rows // chunk
     chunks = outer * per
     bf, f32 = jnp.bfloat16, jnp.float32
-    pos = lax.broadcasted_iota(jnp.int32, (tok, 1), 0)
-    incoming = upstream * (pos < lengths[0]).astype(bf)
+    part = min(128, chunk)
+    parts_g, per_g = rows * outer // part, rows // part
     dma = pltpu.SemaphoreType.DMA
     hbm = pl.BlockSpec(memory_space=pl.ANY)
     vmem = pl.BlockSpec(memory_space=pltpu.VMEM)
     flops = 4 * tok_group * draft * depth
-    normed, gw, gg = pl.pallas_call(
+    normed, own, others, gg = pl.pallas_call(
         functools.partial(kernel, dp, tp),
         out_shape=(jax.ShapeDtypeStruct((tok, draft), bf),
-                   jax.ShapeDtypeStruct((layers, per, chunk, slab), f32),
+                   jax.ShapeDtypeStruct((layers, per_g, part, slab), bf),
+                   jax.ShapeDtypeStruct((max(1, outer - 1), layers, per_g, part, slab), bf),
                    jax.ShapeDtypeStruct((outer, INNER, per, 1, chunk), f32)),
-        in_specs=[hbm, hbm, hbm, vmem],
-        out_specs=(hbm, vmem, vmem),
+        in_specs=[hbm, hbm, hbm, vmem, pl.BlockSpec(memory_space=pltpu.SMEM)],
+        out_specs=(hbm, hbm, hbm, vmem),
         scratch_shapes=[
             pltpu.VMEM((layers, tp, INNER, tok, slab), bf),
             pltpu.VMEM((layers, chunks, chunk, slab), bf),
@@ -376,9 +388,10 @@
             pltpu.VMEM((INNER, chunks, tok, chunk), f32),
             pltpu.VMEM((INNER, outer, tok, rows), bf),
             pltpu.VMEM((INNER, outer, tok, rows), bf),
-            pltpu.VMEM((chunks, tp, chunk, INNER * tok), bf),
-            pltpu.VMEM((max(1, chunks - per), layers, chunk, slab), bf),
-            pltpu.VMEM((max(1, chunks - per), layers, chunk, slab), bf),
+            pltpu.VMEM((parts_g, tp, part, INNER * tok), bf),
+            pltpu.VMEM((max(1, parts_g - per_g), layers, part, slab), bf),
+            pltpu.VMEM((layers, per_g, part, slab), bf),
+            pltpu.VMEM((tok, draft), bf),
             pltpu.VMEM((2 * INNER, tok), f32),
             pltpu.VMEM((INNER, 2 * INNER, tok), f32),
             pltpu.VMEM((chunks, chunk), f32),
@@ -391,9 +404,10 @@
             dma((INNER, outer)), dma((INNER, outer)),
             dma((tp, chunks, INNER // 2)), dma((tp, chunks, INNER // 2)),
             dma((INNER,)), dma((INNER,)),
-            dma((chunks, 2, tp)), dma((chunks, 2, tp)),
+            dma((parts_g, 2, tp)), dma((parts_g, 2, tp)),
             dma((INNER, outer)), dma((INNER, outer)),
-            dma((chunks, layers)), dma((chunks, layers)),
+            dma((max(1, parts_g - per_g), layers)), dma((max(1, outer - 1), layers, per_g)),
+            dma((layers, per_g)),
             dma((tp,)), dma((tp,)),
             dma((outer,)), dma((outer,)),
             dma((INNER,)), dma((INNER,)),
@@ -403,8 +417,11 @@
         cost_estimate=pl.CostEstimate(flops=flops, bytes_accessed=8 * tok_group * depth,
                                       transcendentals=0),
     )(hidden_states.transpose(1, 0, 2).reshape(layers, tp, tok, slab),
-      fc_weight.transpose(1, 0, 2).reshape(layers, per, chunk, slab), incoming,
-      norm_gain.reshape(outer, INNER, per, 1, chunk))
+      fc_weight.transpose(1, 0, 2).reshape(layers, per, chunk, slab), upstream,
+      norm_gain.reshape(outer, INNER, per, 1, chunk), lengths)
+    gw = own.astype(f32)
+    for r in range(outer - 1):
+        gw = gw + others[r].astype(f32)
     return normed, gw.reshape(layers, rows, slab).transpose(1, 0, 2), gg.reshape(draft)
 
 

time: 232 us -> 220 us (0.948)
  Pallas kernels: 218 us -> 210 us
  local copies, waits for them, and re-layouts: 9.52 us -> 1.59 us
  other arithmetic: 2.34 us -> 7.13 us
    pallas_call x1, Pallas kernels: 218 us -> 210 us  [body(): pl.pallas_call(functools.partial(kernel, dp, tp), out_shape=(jax.ShapeDty...]
    unnamed x5 -> x6, local copies, waits for them, and re-layouts: 9.52 us -> 1.59 us
    add x0 -> x1, other arithmetic: none -> 7.13 us  [body(): gw = gw + others[r].astype(f32)]
    mul x1 -> x0, other arithmetic: 2.33 us -> none  [body(): incoming = upstream * (pos < lengths[0]).astype(bf)]
where the time goes in v3:
time: 220 us
  Pallas kernels  210 us (95%)
  other arithmetic  7.13 us (3%)
    pallas_call x1, Pallas kernels, body(): pl.pallas_call(functools.partial(kernel, dp, tp), out_shape=(jax.ShapeDty...  210 us
    add x1, other arithmetic, body(): gw = gw + others[r].astype(f32)  7.13 us

profile of v3, /device:TPU:0, one launch (start us, length us, event | category | flops | bytes accessed | tf_op | source)
XLA Modules:
  0.0 219.6 jit_solution(10186211913749564754)
XLA Ops:
  1.3 209.6 %shard_map.76 = (bf16[128,4096]{1,0:T(8,128)(2,1)}, bf16[3,4,128,1024]{3,2,1,0:T(8,128)(2,1)}, bf16[1,3,4,128,1024]{4,3,2,1,0:T(8,128)(2,1)}, f32[2,4,2,1,256]{4,3,2,1,0:T(1,128)}) custom-call(bf16[3,4,128,1024]{3,2,1,0:T(8,128)(2,1)} %bitcast.16, bf16[3,2,256,1024]{3,2,1,0:T(8,128)(2,1)} %bitcast.17, bf16[128,4096]{1,0:T(8,128)(2,1)} %up_ref.1, ...), custom_call_target="tpu_custom_call" | custom-call | flops 25769803776 | bytes 12582912 | tf_op jit(solution)/shard_map/pallas_call | solution.py:375
  210.9 0.0 copy-start
  210.9 0.0 copy-start.1
  210.9 7.1 %convert_add_fusion = f32[3,4,128,1024]{3,2,1,0:T(8,128)} fusion(bf16[3,4,128,1024]{3,2,1,0:T(8,128)(2,1)} %get-tuple-element.8, bf16[1,3,4,128,1024]{4,3,2,1,0:T(8,128)(2,1)} %get-tuple-element.9), kind=kLoop, calls=%fused_computation | loop fusion | flops 4718592 | bytes 12582912 | tf_op jit(solution)/shard_map/add | solution.py:424
  218.0 0.0 copy-done
  218.0 1.0 copy.11
  219.0 0.0 copy-done.1
  219.0 0.6 copy.12
Async XLA Ops:
  210.9 7.2 %copy-start = (bf16[128,4096]{1,0:T(8,128)(2,1)S(1)}, bf16[128,4096]{1,0:T(8,128)(2,1)}, u32[]{:S(2)}) copy-start(bf16[128,4096]{1,0:T(8,128)(2,1)} %get-tuple-element.14) | copy-start | bytes 3145732
  210.9 8.1 %copy-start.1 = (f32[2,4,2,1,256]{4,3,2,1,0:T(1,128)S(1)}, f32[2,4,2,1,256]{4,3,2,1,0:T(1,128)}, u32[]{:S(2)}) copy-start(f32[2,4,2,1,256]{4,3,2,1,0:T(1,128)} %get-tuple-element.10) | copy-start | bytes 49156

commit v4 on v3

--- a/solution.py
+++ b/solution.py
@@ -218,23 +218,28 @@
         def _():
             ag_copy(wc, t, -1).start()
 
-    def ag_take(wc):
-        for k in range(1, tp):
-            @pl.when(t - k >= 0)
+    def ag_take(wc, k):
+        @pl.when(t - k >= 0)
+        def _():
+            ag_copy(wc, (t - k + tp) % tp, 1).wait_recv()
+
+            @pl.when(t < tp - 1)
             def _():
-                ag_copy(wc, (t - k + tp) % tp, 1).wait_recv()
-
-                @pl.when(t < tp - 1)
-                def _():
-                    ag_copy(wc, (t - k + tp) % tp, 1).start()
-
-            @pl.when(t + k < tp)
+                ag_copy(wc, (t - k + tp) % tp, 1).start()
+
+        @pl.when(t + k < tp)
+        def _():
+            ag_copy(wc, (t + k) % tp, -1).wait_recv()
+
+            @pl.when(t > 0)
             def _():
-                ag_copy(wc, (t + k) % tp, -1).wait_recv()
-
-                @pl.when(t > 0)
-                def _():
-                    ag_copy(wc, (t + k) % tp, -1).start()
+                ag_copy(wc, (t + k) % tp, -1).start()
+
+    def ag_step(n):
+        for k in range(tp - 1, 0, -1):
+            m = n + tp - 1 - k
+            if 0 <= m < parts_g:
+                ag_take(order[m], k)
 
     def ag_done(wc):
         for k in range(tp):
@@ -261,7 +266,7 @@
             grad = inverse[s] * (incoming * gain - scaled * proj[s])
             gmt[g, t, :, s * tok:(s + 1) * tok] = jnp.swapaxes(grad, 0, 1).astype(jnp.bfloat16)
         gg[wc:wc + 1, sub] = own
-        if g in order[:2]:
+        if g in order[:tp - 1]:
             ag_own(g)
 
     for s in range(1, INNER):
@@ -310,10 +315,12 @@
         return rdma(gstage.at[k, l], grecv.at[outer - r - 1, l, k % per_g], gs.at[k, l],
                     gr.at[outer - r - 1, l, k % per_g], far(r))
 
+    for n in range(2 - tp, 0):
+        ag_step(n)
     for n, g in enumerate(order):
-        ag_take(g)
-        if n + 2 < parts_g:
-            ag_own(order[n + 2])
+        ag_step(n)
+        if n + tp - 1 < parts_g:
+            ag_own(order[n + tp - 1])
         for l in range(layers):
             def step(k, carry):
                 cols = pl.ds(pl.multiple_of(k * tile, 128), tile)

time: 220 us -> 221 us (level)
  no operation moved by 1% of the time
where the time goes in v4:
time: 221 us
  Pallas kernels  211 us (95%)
  other arithmetic  7.13 us (3%)
    pallas_call x1, Pallas kernels, body(): pl.pallas_call(functools.partial(kernel, dp, tp), out_shape=(jax.ShapeDty...  211 us
    add x1, other arithmetic, body(): gw = gw + others[r].astype(f32)  7.13 us

profile of v4, /device:TPU:0, one launch (start us, length us, event | category | flops | bytes accessed | tf_op | source)
XLA Modules:
  0.0 221.0 jit_solution(16833577198514745990)
XLA Ops:
  1.3 211.0 %shard_map.76 = (bf16[128,4096]{1,0:T(8,128)(2,1)}, bf16[3,4,128,1024]{3,2,1,0:T(8,128)(2,1)}, bf16[1,3,4,128,1024]{4,3,2,1,0:T(8,128)(2,1)}, f32[2,4,2,1,256]{4,3,2,1,0:T(1,128)}) custom-call(bf16[3,4,128,1024]{3,2,1,0:T(8,128)(2,1)} %bitcast.16, bf16[3,2,256,1024]{3,2,1,0:T(8,128)(2,1)} %bitcast.17, bf16[128,4096]{1,0:T(8,128)(2,1)} %up_ref.1, ...), custom_call_target="tpu_custom_call" | custom-call | flops 25769803776 | bytes 12582912 | tf_op jit(solution)/shard_map/pallas_call | solution.py:382
  212.3 0.0 copy-start
  212.3 0.0 copy-start.1
  212.3 7.1 %convert_add_fusion = f32[3,4,128,1024]{3,2,1,0:T(8,128)} fusion(bf16[3,4,128,1024]{3,2,1,0:T(8,128)(2,1)} %get-tuple-element.8, bf16[1,3,4,128,1024]{4,3,2,1,0:T(8,128)(2,1)} %get-tuple-element.9), kind=kLoop, calls=%fused_computation | loop fusion | flops 4718592 | bytes 12582912 | tf_op jit(solution)/shard_map/add | solution.py:431
  219.4 0.0 copy-done
  219.4 1.0 copy.11
  220.4 0.0 copy-done.1
  220.4 0.6 copy.12
Async XLA Ops:
  212.3 7.2 %copy-start = (bf16[128,4096]{1,0:T(8,128)(2,1)S(1)}, bf16[128,4096]{1,0:T(8,128)(2,1)}, u32[]{:S(2)}) copy-start(bf16[128,4096]{1,0:T(8,128)(2,1)} %get-tuple-element.14) | copy-start | bytes 3145732
  212.3 8.1 %copy-start.1 = (f32[2,4,2,1,256]{4,3,2,1,0:T(1,128)S(1)}, f32[2,4,2,1,256]{4,3,2,1,0:T(1,128)}, u32[]{:S(2)}) copy-start(f32[2,4,2,1,256]{4,3,2,1,0:T(1,128)} %get-tuple-element.10) | copy-start | bytes 49156
